TPU v7x, 1024 devices: a whole 4x8x16 slice. The times are simulated.
1024 devices in a mesh: ep: 16 (over z_lo, x), fsdp: 16 (over y, core), dp: 4 (over z_hi).
Axes of the slice: x: 4, y: 8, z: 16 (z_hi: 4, z_lo: 4; z = z_hi * 4 + z_lo), core: 2. Of those that a mesh axis runs over, the one named last changes fastest.
Arguments:
- learner_in: bfloat16 [64, 2048, 1024], P(('ep', 'dp'), 'fsdp'), may hold values from -0.125 to 0.125
- learner_out: bfloat16 [64, 512, 2048], P(('ep', 'dp'), None, 'fsdp'), may hold values from -0.25 to 0.25
- placement: int32 [64], replicated, may hold values from 0 to 63, each once
- hidden: bfloat16 [8192, 2048], P(('ep', 'fsdp', 'dp')), may hold values from -6 to 6
- norm_gain: float32 [2048], replicated, may hold values from 0.1 to 1.9
- expert_ids: int32 [1, 8192, 10], P(None, ('ep', 'fsdp', 'dp')), may hold values from 0 to 63, all different within a row; in each aligned block of 8 rows (0 to 7, 8 to 15, ..., all dimensions but the last counted through in order) at most 2 rows name the same one
- gate_weights: float32 [1, 8192, 10], P(None, ('ep', 'fsdp', 'dp')), may hold values from 0.1 to 0.5
Outputs:
- rollout_in: bfloat16 [64, 2048, 1024], P(('ep', 'dp'))
- rollout_out: bfloat16 [64, 512, 2048], P(('ep', 'dp'))
- final_rows: bfloat16 [8192, 2048], P(('ep', 'fsdp', 'dp'))
Inputs may be any that keep to these rules, and one draw needn't show every extreme that they name: `placement`: each expert id appears in exactly one position. `expert_ids`: the 10 ids of a row differ. In each step, no id is named by more than 2 rows of one device; some id reaches 2.
All inputs are finite; a program needn't handle non-finite values.
Results may differ from a plain program's by a relative error of at most 0.0051.
Values may be sent and summed in bfloat16 or wider, within the bound.
A program may use at most 64 MiB of HBM per device.

v0:
```python
import jax
import jax.numpy as jnp
from jax import lax
from jax.sharding import PartitionSpec as P

QBLOCK = 128
CAP = 2


scale_table = [2.0**k for k in range(-40, 16)]
binade_table = [2.0 ** (-k) for k in range(15)]


def block_levels(weights):
    count, height, span = weights.shape
    blocks = weights.astype(jnp.float32).reshape(
        count, height // QBLOCK, QBLOCK, span // QBLOCK, QBLOCK
    )
    peak = jnp.max(jnp.abs(blocks), axis=(2, 4))
    candidates = jnp.asarray(scale_table, jnp.float32)
    scales = jnp.max(
        jnp.where(peak[..., None] >= candidates, candidates, candidates[0]), axis=-1
    ).astype(jnp.bfloat16)
    quotient = blocks / scales.astype(jnp.float32)[:, :, None, :, None]
    magnitude = jnp.abs(quotient)
    binade = jnp.full_like(magnitude, binade_table[-1])
    for threshold in binade_table[:-1]:
        binade = jnp.maximum(binade, jnp.where(magnitude >= threshold, threshold, 0.0))
    rounded = jnp.floor(magnitude / binade * 8.0 + 0.5) * binade * 0.125
    levels = (jnp.sign(quotient) * rounded).astype(jnp.bfloat16)
    return (levels.reshape(count, height, span), scales)


def restore(levels, scales):
    count, height, span = levels.shape
    blocks = levels.reshape(count, height // QBLOCK, QBLOCK, span // QBLOCK, QBLOCK)
    return (blocks * scales[:, :, None, :, None]).reshape(count, height, span)


def per_device(learner_in, learner_out, placement, hidden, norm_gain, expert_ids, gate_weights):
    levels_in, scales_in = block_levels(learner_in)
    levels_out, scales_out = block_levels(learner_out)
    full_in, full_out, whole_scales_in, whole_scales_out = (
        lax.all_gather(levels_in, "fsdp", axis=1, tiled=True),
        lax.all_gather(levels_out, "fsdp", axis=2, tiled=True),
        lax.all_gather(scales_in, "fsdp", axis=1, tiled=True),
        lax.all_gather(scales_out, "fsdp", axis=2, tiled=True),
    )
    rollout_in = restore(full_in, whole_scales_in)
    rollout_out = restore(full_out, whole_scales_out)
    owners = lax.axis_size("ep") * lax.axis_size("dp")
    local = rollout_in.shape[0]
    inner_width = rollout_out.shape[1]
    row_count, width = hidden.shape
    steps, _, top = expert_ids.shape
    experts = placement.shape[0]
    capacity = CAP
    column = jnp.arange(experts, dtype=jnp.int32)
    targets = jnp.arange(experts * capacity, dtype=jnp.int32)
    state = hidden
    xfull = state.astype(jnp.float32)
    normed = (
        xfull * lax.rsqrt(jnp.mean(xfull * xfull, axis=-1, keepdims=True) + 1e-06) * norm_gain
    ).astype(jnp.bfloat16)
    lookup = (expert_ids[0][..., None] == column).astype(jnp.int32)
    slot = jnp.sum(lookup * placement, axis=-1).reshape(-1)
    onehot = (slot[:, None] == column[None, :]).astype(jnp.int32)
    rank = jnp.sum((jnp.cumsum(onehot, axis=0) - onehot) * onehot, axis=1)
    target = slot * capacity + rank
    select = (targets[:, None] == target[None, :]).astype(jnp.bfloat16)
    source = jnp.repeat(normed, top, axis=0)
    outgoing = jnp.dot(select, source, preferred_element_type=jnp.float32).astype(jnp.bfloat16)
    outgoing = outgoing.reshape(owners, local, capacity, width)
    arrived = lax.all_to_all(outgoing, ("ep", "dp"), split_axis=0, concat_axis=0, tiled=True)
    projected = jnp.einsum(
        "secd,edf->secf", arrived, rollout_in, preferred_element_type=jnp.float32
    )
    activated = (jax.nn.silu(projected[..., :inner_width]) * projected[..., inner_width:]).astype(
        jnp.bfloat16
    )
    answers = jnp.einsum(
        "secf,efd->secd", activated, rollout_out, preferred_element_type=jnp.float32
    ).astype(jnp.bfloat16)
    returned = lax.all_to_all(answers, ("ep", "dp"), split_axis=0, concat_axis=0, tiled=True)
    back_rows = returned.reshape(experts * capacity, width)
    picked = jnp.einsum("sp,sd->pd", select, back_rows, preferred_element_type=jnp.float32).reshape(
        row_count, top, width
    )
    combined = jnp.sum(gate_weights[0][..., None] * picked, axis=1)
    state = (xfull + combined).astype(jnp.bfloat16)
    return (rollout_in, rollout_out, state)


def solution(mesh):
    in_specs = (
        P(("ep", "dp"), "fsdp", None),
        P(("ep", "dp"), None, "fsdp"),
        P(),
        P(("ep", "fsdp", "dp"), None),
        P(),
        P(None, ("ep", "fsdp", "dp"), None),
        P(None, ("ep", "fsdp", "dp"), None),
    )
    out_specs = (
        P(("ep", "dp"), None, None),
        P(("ep", "dp"), None, None),
        P(("ep", "fsdp", "dp"), None),
    )
    return jax.shard_map(
        per_device, mesh=mesh, in_specs=in_specs, out_specs=out_specs, check_vma=False
    )
```

profile of v0, /device:TPU:64, one launch (start us, length us, event | category | flops | bytes accessed | tf_op | source)
XLA Modules:
  0.0 190.6 jit_solution(8293335583791452557)
XLA Ops:
  7.2 0.0 all-gather.6.cloned.1.call-start
  7.2 1.0 fusion.11
  8.2 0.1 bitcast_reduce_fusion.1
  8.3 0.8 select_reduce_fusion.3
  9.2 0.1 broadcast_bitcast_fusion.1
  9.3 2.2 %multiply_convert_fusion.1 = bf16[1,512,128]{2,1,0:T(8,128)(2,1)} fusion(bf16[1,512,128]{2,1,0:T(8,128)(2,1)} %param.10, f32[512]{0:T(512)S(1)} %broadcast_bitcast_fusion.1), kind=kLoop, calls=%fused_computation.28 | loop fusion | flops 3538944 | bytes 264192 | tf_op jit(solution)/shard_map/convert_element_type | solution.py:30
  11.4 0.0 all-gather.6.cloned.1.call-update
  11.5 0.0 all-gather.4.cloned.1.call-start
  11.5 1.0 fusion.8
  12.5 0.1 bitcast_reduce_fusion
  12.6 0.8 select_reduce_fusion.2
  13.5 0.1 broadcast_bitcast_fusion
  13.5 2.7 %multiply_convert_fusion = bf16[1,128,1024]{2,1,0:T(8,128)(2,1)} fusion(bf16[1,128,1024]{2,1,0:T(8,128)(2,1)} %param.9, f32[1024]{0:T(1024)S(1)} %broadcast_bitcast_fusion), kind=kLoop, calls=%fused_computation.14 | loop fusion | flops 7077888 | bytes 528384 | tf_op jit(solution)/shard_map/convert_element_type | solution.py:30
  16.2 0.0 all-gather.4.cloned.1.call-update
  16.3 0.8 copy.24
  17.0 1.0 select_reduce_fusion.1
  18.0 0.1 copy.25
  18.1 0.1 reshape.414
  18.2 0.9 fusion.15
  19.1 0.8 fusion.17
  20.0 0.1 reshape.417
  20.1 0.1 fusion.19
  20.2 0.1 reduce_window_sum.11
  20.3 0.2 select_reduce_fusion
  20.5 0.3 convolution_convert_fusion.1
  20.8 1.2 reshape.418
  21.9 21.4 %all-to-all-start = ((bf16[64,1,2,2048]{3,2,1,0:T(2,128)(2,1)}), bf16[64,1,2,2048]{3,2,1,0:T(2,128)(2,1)S(1)}, u32[]{:S(2)}, u32[]{:S(2)}) async-start(bf16[64,1,2,2048]{3,2,1,0:T(2,128)(2,1)} %bitcast.14), calls=%async_computation | async-start | bytes 1048576 | tf_op jit(solution)/shard_map/all_to_all | solution.py:74
  43.4 1.3 dynamic-slice
  45.3 0.2 dynamic-update-slice
  45.6 27.1 %all-reduce = bf16[128]{0:T(256)(128)(2,1)S(1)} all-reduce(bf16[128]{0:T(256)(128)(2,1)S(1)} %dynamic-update-slice), channel_id=2, replica_groups=mesh['ep'=16,'fsdp'=16,'dp'=4] {'fsdp'}, use_global_device_ids=true, to_apply=%add | all-reduce | flops 128 | bytes 512
  72.7 0.1 mul.146
  72.8 2.6 %mul.147 = bf16[16,128,8,128]{3,2,1,0:T(8,128)(2,1)} broadcast(bf16[16,8]{1,0:T(8,128)(2,1)S(1)} %mul.146), dimensions={0,2} | broadcast | bytes 4194560 | tf_op jit(solution)/shard_map/mul | solution.py:37
  75.4 7.3 %mul.148 = bf16[1,2048,1024]{2,1,0:T(8,128)(2,1)} reshape(bf16[16,128,8,128]{3,2,1,0:T(8,128)(2,1)} %mul.147) | data formatting | bytes 8388608 | tf_op jit(solution)/shard_map/mul | solution.py:37
  82.7 14.0 %all_gather.15 = bf16[1,4,16]{1,0,2:T(2,128)(2,1)S(1)} all-gather(bf16[1,4,1]{1,0,2:T(2,128)(2,1)S(1)} %bitcast.51), channel_id=1, replica_groups=mesh['ep'=16,'fsdp'=16,'dp'=4] {'fsdp'}, dimensions={2}, use_global_device_ids=true | all-gather | bytes 136 | tf_op jit(solution)/shard_map/all_gather | solution.py:47
  96.7 0.1 copy.23
  96.8 1.7 mul.156
  98.5 2.8 %mul.157 = bf16[1,512,2048]{2,1,0:T(8,128)(2,1)S(1)} reshape(bf16[4,128,16,128]{3,2,1,0:T(8,128)(2,1)} %mul.156) | data formatting | bytes 4194304 | tf_op jit(solution)/shard_map/mul | solution.py:37
  101.3 0.0 all-gather.6.cloned.1.call-done
  101.3 3.7 %mul.158 = bf16[1,512,2048]{2,1,0:T(8,128)(2,1)} multiply(bf16[1,512,2048]{2,1,0:T(8,128)(2,1)} %all-gather.6.cloned.1.call-done, bf16[1,512,2048]{2,1,0:T(8,128)(2,1)S(1)} %mul.157) | non-fusion elementwise | flops 1048576 | bytes 6291456 | tf_op jit(solution)/shard_map/mul | solution.py:37
  105.1 14.8 %all-gather.4.cloned.1.call-done = bf16[1,2048,1024]{2,1,0:T(8,128)(2,1)} async-done(((bf16[1,128,1024]{2,1,0:T(8,128)(2,1)}), bf16[1,2048,1024]{2,1,0:T(8,128)(2,1)}) %all-gather.4.cloned.1.call-update) | async-done | bytes 4194320 | tf_op jit(solution)/shard_map/all_gather | solution.py:44
  119.8 7.6 %mul.149 = bf16[1,2048,1024]{2,1,0:T(8,128)(2,1)} multiply(bf16[1,2048,1024]{2,1,0:T(8,128)(2,1)} %all-gather.4.cloned.1.call-done, bf16[1,2048,1024]{2,1,0:T(8,128)(2,1)} %mul.148) | non-fusion elementwise | flops 2097152 | bytes 12582912 | tf_op jit(solution)/shard_map/mul | solution.py:37
  127.4 0.0 copy-start
  127.4 0.0 all-to-all-done
  127.4 3.1 %fusion.5 = f32[64,1,2,1024]{3,0,2,1:T(8,128)S(1)} fusion(bf16[1,2048,1024]{2,1,0:T(8,128)(2,1)} %mul.149, bf16[64,1,2,2048]{3,2,1,0:T(2,128)(2,1)S(1)} %all-to-all-done), kind=kOutput, calls=%fused_computation.8 | convolution fusion | flops 536870912 | bytes 5242880 | tf_op jit(solution)/shard_map/secd,edf->secf/dot_general | solution.py:75
  130.5 0.0 copy-done
  130.5 0.0 copy-start.2
  130.5 0.0 copy-start.1
  130.5 0.5 fusion.2
  131.0 1.3 copy.28
  132.3 16.1 %all-to-all-start.1 = ((bf16[64,1,2,2048]{3,2,1,0:T(2,128)(2,1)}), bf16[64,1,2,2048]{3,2,1,0:T(2,128)(2,1)S(1)}, u32[]{:S(2)}, u32[]{:S(2)}) async-start(bf16[64,1,2,2048]{3,2,1,0:T(2,128)(2,1)} %copy.28), calls=%async_computation.1 | async-start | bytes 1048576 | tf_op jit(solution)/shard_map/all_to_all | solution.py:84
  148.5 0.1 iota_compare_fusion.4
  148.6 34.0 %all-to-all-done.1 = bf16[64,1,2,2048]{3,2,1,0:T(2,128)(2,1)S(1)} async-done(((bf16[64,1,2,2048]{3,2,1,0:T(2,128)(2,1)}), bf16[64,1,2,2048]{3,2,1,0:T(2,128)(2,1)S(1)}, u32[]{:S(2)}, u32[]{:S(2)}) %all-to-all-start.1) | async-done | bytes 524320 | tf_op jit(solution)/shard_map/all_to_all | solution.py:84
  182.6 0.2 reshape.431
  182.8 0.0 copy-done.2
  182.8 0.4 fusion.4
  183.1 0.0 copy-done.1
  183.2 0.6 fusion.18
  (7 shorter events, 0.1 us)
Async XLA Ops:
  7.2 94.2 %all-gather.6.cloned.1.call-start = ((), (), s32[]{:S(2)}) async-start(), calls=%async_computation.3 | async-start | bytes 2228224 | tf_op jit(solution)/shard_map/all_gather | solution.py:45
  11.5 108.4 %all-gather.4.cloned.1.call-start = ((), (), s32[]{:S(2)}) async-start(), calls=%async_computation.2 | async-start | bytes 4456448 | tf_op jit(solution)/shard_map/all_gather | solution.py:44
  21.9 105.5 %all-to-all-start = ((bf16[64,1,2,2048]{3,2,1,0:T(2,128)(2,1)}), bf16[64,1,2,2048]{3,2,1,0:T(2,128)(2,1)S(1)}, u32[]{:S(2)}, u32[]{:S(2)}) async-start(bf16[64,1,2,2048]{3,2,1,0:T(2,128)(2,1)} %bitcast.14), calls=%async_computation | async-start | bytes 1048576 | tf_op jit(solution)/shard_map/all_to_all | solution.py:74
  127.4 3.1 %copy-start = (bf16[1,512,2048]{2,1,0:T(8,128)(2,1)S(1)}, bf16[1,512,2048]{2,1,0:T(8,128)(2,1)}, u32[]{:S(2)}) copy-start(bf16[1,512,2048]{2,1,0:T(8,128)(2,1)} %mul.158) | copy-start | bytes 6291460
  130.5 52.3 %copy-start.2 = (f32[1,8,10]{2,1,0:T(8,128)S(1)}, f32[1,8,10]{2,1,0:T(8,128)}, u32[]{:S(2)}) copy-start(f32[1,8,10]{2,1,0:T(8,128)} %param.15) | copy-start | bytes 964
  130.5 52.6 %copy-start.1 = (bf16[8,2048]{1,0:T(8,128)(2,1)S(1)}, bf16[8,2048]{1,0:T(8,128)(2,1)}, u32[]{:S(2)}) copy-start(bf16[8,2048]{1,0:T(8,128)(2,1)} %param.12) | copy-start | bytes 98308
  132.3 50.2 %all-to-all-start.1 = ((bf16[64,1,2,2048]{3,2,1,0:T(2,128)(2,1)}), bf16[64,1,2,2048]{3,2,1,0:T(2,128)(2,1)S(1)}, u32[]{:S(2)}, u32[]{:S(2)}) async-start(bf16[64,1,2,2048]{3,2,1,0:T(2,128)(2,1)} %copy.28), calls=%async_computation.1 | async-start | bytes 1048576 | tf_op jit(solution)/shard_map/all_to_all | solution.py:84
Sparse Core Ops, SparseCore 0:
  11.6 55.7 all-gather.5
  70.1 49.7 all-gather.3
where the time goes:
time: 191 us
  waiting for transfers between devices  48.8 us (26%)
  blocking collectives  41.1 us (22%)
  starting transfers between devices  37.6 us (20%)
  other arithmetic  23.9 us (13%)
  local copies, waits for them, and re-layouts  20.1 us (11%)
  between operations  14.9 us (8%)
  matrix products  4.16 us (2%)
    all_to_all x1, waiting for transfers between devices, per_device(): lax.all_to_all(answers, ('ep', 'dp'), split_axis=0, concat_axis=0, tiled=...  34 us
    unnamed x1, blocking collectives  27.1 us
    all_to_all x1, starting transfers between devices, per_device(): lax.all_to_all(outgoing, ('ep', 'dp'), split_axis=0, concat_axis=0, tiled...  21.4 us
    all_to_all x1, starting transfers between devices, per_device(): lax.all_to_all(answers, ('ep', 'dp'), split_axis=0, concat_axis=0, tiled=...  16.1 us
    all_gather x1, waiting for transfers between devices, per_device(): lax.all_gather(levels_in, 'fsdp', axis=1, tiled=True)  14.8 us
    mul x5, local copies, waits for them, and re-layouts, restore(): return (blocks * scales[:, :, None, :, None]).reshape(count, height, span)  14.5 us
    all_gather x1, blocking collectives, per_device(): lax.all_gather(scales_out, 'fsdp', axis=2, tiled=True)  14 us
    mul x2, other arithmetic, restore(): return (blocks * scales[:, :, None, :, None]).reshape(count, height, span)  11.3 us
  transfers between devices with their start and end apart: 4, of which 2 were waited for; matrix products, arithmetic and copies ran while one was open for 20% of the time, Pallas kernels for 0%

commit v1 on v0

v1 whole, which is shorter than its diff:
```python
import jax
import jax.numpy as jnp
from jax import lax
from jax.experimental import pallas as pl
from jax.experimental.pallas import tpu as pltpu
from jax.sharding import PartitionSpec as P

MESH = pl.DeviceIdType.MESH
BF, F32 = jnp.bfloat16, jnp.float32
BLOCK = 128
CHUNKS = ((0, 1, -1), (2, -2), (3, -3, 4))
RELAYS = (3, -3, 6, -6)
HEADS = (0, 3, -3, 6, -6)


def remote(src, dst, send_sem, recv_sem, device):
    return pltpu.make_async_remote_copy(
        src_ref=src,
        dst_ref=dst,
        send_sem=send_sem,
        recv_sem=recv_sem,
        device_id=device,
        device_id_type=MESH,
    )


def dot(a, b):
    return jnp.dot(a, b, preferred_element_type=F32)


def dot_t(a, b):
    return lax.dot_general(a, b, (((1,), (1,)), ((), ())), preferred_element_type=F32)


def iota(shape, dim):
    return lax.broadcasted_iota(jnp.int32, shape, dim)


def block_scales(peaks):
    scales = jnp.full_like(peaks, 2.0**-40)
    for k in range(-39, 16):
        scales = jnp.where(peaks >= 2.0**k, 2.0**k, scales)
    return scales


def quantized(block, scale):
    nudged = block * (1.0 + 2.0**-10)
    spread = nudged * (2.0**20 + 1.0)
    coarse = spread - (spread - nudged)
    anchor = scale * 96.0
    fine = (nudged + anchor) - anchor
    return jnp.where(jnp.abs(block) >= scale * 2.0**-14, coarse, fine).astype(BF)


def fold(a):
    half = a.shape[1] // 2
    return jnp.concatenate([a[:, :half], a[:, half:]], axis=0)


def kernel(
    lin_hbm, lout_hbm, place_hbm, hid_hbm, gain_hbm, ids_hbm, gates_hbm,
    rin, rout, final,
    lin, lout, place, hid, gain, ids, gates,
    bundles, outgoing, arrived, acc, merge,
    ans, back, leaf_out, leaf_in, far_out, far_in, relay_out, relay_in,
    load_sem,
    in_ss, in_rs, out_ss, out_rs, insib_ss, insib_rs, outsib_ss, outsib_rs,
    z_ss, z_rs, x_ss, x_rs, bx_ss, bx_rs, leaf_ss, leaf_rs, far_ss, far_rs, rel_ss, rel_rs,
):
    ep, dp, fs = lax.axis_index("ep"), lax.axis_index("dp"), lax.axis_index("fsdp")
    x, z = ep % 4, dp * 4 + ep // 4
    y, core = fs // 2, fs % 2

    def xz(dx, dz):
        tx, tz = (x + dx + 4) % 4, (z + dz + 16) % 16
        return {"ep": (tz % 4) * 4 + tx, "dp": tz // 4}

    up, down = {"fsdp": (fs + 2) % 16}, {"fsdp": (fs + 14) % 16}
    sibling = {"fsdp": fs + 1 - 2 * core}

    loads = []
    for i, (s, d) in enumerate((
        (lin_hbm, lin), (hid_hbm, hid), (gain_hbm, gain), (ids_hbm, ids),
        (gates_hbm, gates), (place_hbm, place), (lout_hbm, lout),
    )):
        c = pltpu.make_async_copy(s, d, load_sem.at[i])
        c.start()
        loads.append(c)

    barrier = pltpu.get_barrier_semaphore()
    peers = [up, down, sibling] + [xz(d, 0) for d in (1, 2, 3)]
    peers += [xz(0, d) for d in (1, -1, 2, -2, 3, -3, 6, -6)]
    for peer in peers:
        pl.semaphore_signal(barrier, inc=1, device_id=peer, device_id_type=MESH)

    sends = []

    def send(c):
        c.start()
        sends.append(c)
        return c

    def chip_of(distance):
        return (y + distance + 8) % 8

    def in_ref(distance, k, c):
        row = (chip_of(distance) * 2 + c) * 128 + k * 64
        return rin.at[pl.ds(pl.multiple_of(row, 64), 64), :]

    def out_ref(distance, k, c):
        column = (chip_of(distance) * 2 + c) * 128
        return rout.at[pl.ds(k * 256, 256), pl.ds(pl.multiple_of(column, 128), 128)]

    ring = {}

    class Gather:
        def __init__(self, ref, ss, rs, sib_ss, sib_rs):
            self.ref, self.ss, self.rs, self.sib_ss, self.sib_rs = ref, ss, rs, sib_ss, sib_rs
            self.got, self.sib = {}, {}
            self.n = 0
            self.m = 0

        def push(self, step, k, way):
            held = -step if way == 0 else step
            piece = self.ref(held, k, core)
            c = remote(piece, piece, self.ss.at[self.n], self.rs.at[self.n], up if way == 0 else down)
            self.n += 1
            self.got[(step + 1, k, way)] = send(c)

        def share(self, distance, k):
            piece = self.ref(distance, k, core)
            c = remote(piece, piece, self.sib_ss.at[self.m], self.sib_rs.at[self.m], sibling)
            self.m += 1
            self.sib[(distance, k)] = send(c)

        def arrive(self, step, k, way):
            self.got[(step, k, way)].wait_recv()
            if step < 3 or (step == 3 and k == way):
                self.push(step, k, way)
            distance = -step if way == 0 else step
            self.share(4 if step == 4 else distance, k)

        def ready(self, distance):
            for k in (0, 1):
                self.sib[(distance, k)].wait_recv()

    gin = Gather(in_ref, in_ss, in_rs, insib_ss, insib_rs)
    gout = Gather(out_ref, out_ss, out_rs, outsib_ss, outsib_rs)

    loads[0].wait()
    peaks = []
    for b in range(8):
        peaks.append(jnp.max(jnp.abs(lin[:, b * BLOCK:(b + 1) * BLOCK].astype(F32)), axis=0, keepdims=True))
    peak = jnp.max(jnp.concatenate(peaks, axis=0), axis=1, keepdims=True)
    scales = block_scales(jnp.broadcast_to(peak, (8, 128)))
    own_row = fs * 128
    for b in range(8):
        for r in (0, 64):
            block = lin[r:r + 64, b * BLOCK:(b + 1) * BLOCK].astype(F32)
            rin[pl.ds(pl.multiple_of(own_row + r, 64), 64), b * BLOCK:(b + 1) * BLOCK] = quantized(
                block, scales[b:b + 1, :]
            )
    pl.semaphore_wait(barrier, len(peers))
    for k in (0, 1):
        for way in (0, 1):
            gin.push(0, k, way)
    for k in (0, 1):
        gin.share(0, k)

    for c in loads[1:6]:
        c.wait()
    rows = hid[...].astype(F32)
    normed = rows * lax.rsqrt(jnp.mean(rows * rows, axis=-1, keepdims=True) + 1e-06) * gain[...]
    lane8 = iota((8, 128), 1)
    sub8 = iota((8, 128), 0)
    named = jnp.zeros((8, 128), F32)
    weight = jnp.zeros((8, 128), F32)
    idv, gatev = ids[...], gates[...]
    for k in range(idv.shape[1]):
        hit = jnp.broadcast_to(idv[:, k:k + 1], (8, 128)) == lane8
        named = named + jnp.where(hit, 1.0, 0.0)
        weight = weight + jnp.where(hit, jnp.broadcast_to(gatev[:, k:k + 1], (8, 128)), 0.0)
    earlier = jnp.zeros((8, 128), F32)
    for i in range(7):
        earlier = earlier + jnp.where(sub8 > i, jnp.broadcast_to(named[i:i + 1, :], (8, 128)), 0.0)
    code = named * (1.0 + earlier)
    high = weight.astype(BF).astype(F32)
    low = weight - high
    slot = jnp.broadcast_to(place[...], (128, 64))
    column = ((slot & 3) * 4 + (slot >> 4)) * 4 + ((slot >> 2) & 3)
    move = jnp.where(column == (iota((128, 64), 0) & 63), 1.0, 0.0).astype(BF)
    stacked = jnp.concatenate([code, high, low, jnp.zeros((8, 128), F32)], axis=0)[:, :64].astype(BF)
    moved = dot_t(stacked, move)
    info = jnp.concatenate([
        jnp.where(lane8 < 64, moved[0:8], moved[8:16]),
        jnp.where(lane8 < 64, moved[0:8], moved[16:24]),
    ], axis=0)
    bundles[0, :, 0:1024] = fold(normed).astype(BF)
    bundles[0, :, 1024:1152] = info.astype(BF)

    zgot = {}

    def zsend(held, hop, i):
        there = (held - hop) % 16
        zgot[there] = send(remote(
            bundles.at[held % 16], bundles.at[there], z_ss.at[i], z_rs.at[i], xz(0, hop)
        ))

    for i, hop in enumerate((6, -6, 3, -3)):
        zsend(0, hop, i)
    zsend(0, 1, 4)
    zsend(0, -1, 5)

    loads[6].wait()
    peaks = []
    for b in range(4):
        peaks.append(jnp.max(jnp.abs(lout[b * BLOCK:(b + 1) * BLOCK, :].astype(F32)), axis=0, keepdims=True))
    peak = jnp.max(jnp.concatenate(peaks + peaks, axis=0), axis=1, keepdims=True)
    scales = block_scales(jnp.broadcast_to(peak, (8, 128)))
    own_column = pl.ds(pl.multiple_of(fs * 128, 128), 128)
    for b in range(4):
        for r in (0, 64):
            here = slice(b * BLOCK + r, b * BLOCK + r + 64)
            rout[here, own_column] = quantized(lout[here, :].astype(F32), scales[b:b + 1, :])
    for k in (0, 1):
        gout.share(0, k)

    gin.arrive(1, 0, 0)
    gin.arrive(1, 0, 1)
    number = 6
    for held in (3, -3, 6, -6):
        zgot[held % 16].wait_recv()
        for hop in (1, -1):
            zsend(held, hop, number)
            number += 1
        if held == 6:
            zsend(held, -2, number)
            number += 1
    gin.arrive(1, 1, 0)
    gin.arrive(1, 1, 1)
    gin.arrive(2, 0, 0)
    gin.arrive(2, 0, 1)

    for offset in range(1, 16):
        if offset not in (3, 13, 6, 10):
            zgot[offset].wait_recv()
    every = bundles[...].reshape(256, 1152)
    table, held_rows = every[:, 1024:], every[:, :1024]
    line, lane = iota((128, 128), 0), iota((128, 128), 1)
    target = 4 * z + ((x + (line >> 5)) & 3)
    pick = jnp.where(lane == target, 1.0, 0.0).astype(BF)
    pick_gate = jnp.where(lane == target + 64, 1.0, 0.0).astype(BF)
    line, lane = iota((128, 256), 0), iota((128, 256), 1)
    same = ((line >> 1) & 15) == (lane >> 4)
    chosen = jnp.where(same, dot_t(pick, table), 0.0) == ((line & 1) + 1).astype(F32)
    left = jnp.where(chosen, jnp.where((lane & 8) == 0, 1.0, 0.0), 0.0).astype(BF)
    right = jnp.where(chosen, jnp.where((lane & 8) == 0, 0.0, 1.0), 0.0).astype(BF)
    outgoing[:, 0:1024] = dot(left, held_rows).astype(BF)
    outgoing[:, 1024:2048] = dot(right, held_rows).astype(BF)
    xgot = []
    for dx in (2, 1, 3):
        block = pl.ds(dx * 32, 32)
        xgot.append(send(remote(
            outgoing.at[block, :], arrived.at[block, :], x_ss.at[dx], x_rs.at[dx], xz(dx, 0)
        )))
    arrived[0:32, :] = outgoing[0:32, :]
    line, lane = iota((256, 128), 0), iota((256, 128), 1)
    same = ((lane >> 1) & 15) == (line >> 4)
    chosen = jnp.where(same, dot_t(table, pick), 0.0) == ((lane & 1) + 1).astype(F32)
    merge[...] = jnp.where(chosen, dot_t(table, pick_gate), 0.0).astype(BF)

    gin.arrive(2, 1, 0)
    gin.arrive(2, 1, 1)
    gin.arrive(3, 0, 0)
    gin.arrive(3, 0, 1)
    for c in xgot:
        c.wait_recv()

    def project(distance, first=False):
        gin.ready(distance)
        start = pl.multiple_of(chip_of(distance) * 256, 256)
        part = dot(arrived[:, pl.ds(start, 256)], rin[pl.ds(start, 256), :])
        if first:
            acc[...] = part
        else:
            acc[...] += part

    project(0, True)
    gin.arrive(3, 1, 0)
    gin.arrive(3, 1, 1)
    for k in (0, 1):
        for way in (0, 1):
            gout.push(0, k, way)
    for distance in (1, -1, 2, -2, 3, -3):
        project(distance)
    gin.arrive(4, 0, 0)
    gin.arrive(4, 1, 1)
    project(4)
    gate, lift = acc[:, 0:512], acc[:, 512:1024]
    units = (gate / (1.0 + jnp.exp(-gate)) * lift).astype(BF)

    starts, total = [], 0
    for chunk in CHUNKS:
        starts.append(total)
        total += 256 * len(chunk)
    bgot, lgot, rgot, kept = {}, {}, {}, {}

    def answer(n):
        chunk, start = CHUNKS[n], starts[n]
        for m, distance in enumerate(chunk):
            gout.ready(distance)
            column = pl.multiple_of(chip_of(distance) * 256, 256)
            ans[:, start + 256 * m:start + 256 * (m + 1)] = dot(
                units, rout[:, pl.ds(column, 256)]
            ).astype(BF)
        columns = pl.ds(start, 256 * len(chunk))
        bgot[n] = []
        for dx in (2, 1, 3):
            block = pl.ds(dx * 32, 32)
            bgot[n].append(send(remote(
                ans.at[block, columns], back.at[block, columns],
                bx_ss.at[3 * n + dx - 1], bx_rs.at[3 * n + dx - 1], xz(-dx, 0),
            )))
        back[0:32, start:start + 256 * len(chunk)] = ans[0:32, start:start + 256 * len(chunk)]

    def spread(n):
        start, width = starts[n], 256 * len(CHUNKS[n])
        for c in bgot[n]:
            c.wait_recv()
        sums = dot(merge[...], back[:, start:start + width])

        def part(offset):
            at = (offset % 16) * 16
            return fold(sums[at:at + 8] + sums[at + 8:at + 16])

        half = pl.ds(start // 2, width // 2)
        where = slice(start // 2, start // 2 + width // 2)
        lgot[n] = []
        for j, hop in enumerate((1, -1)):
            for i, head in enumerate(HEADS):
                leaf_out[j, 16 * i:16 * i + 16, where] = part(head + hop).astype(BF)
            lgot[n].append(send(remote(
                leaf_out.at[j, :, half], leaf_in.at[j, :, half],
                leaf_ss.at[2 * n + j], leaf_rs.at[2 * n + j], xz(0, hop),
            )))
        far_out[:, where] = part(8).astype(BF)
        lgot[n].append(send(remote(
            far_out.at[:, half], far_in.at[:, half], far_ss.at[n], far_rs.at[n], xz(0, 2)
        )))
        kept[n] = [part(head) for head in HEADS]

    def relay(n):
        start, width = starts[n], 256 * len(CHUNKS[n])
        half = pl.ds(start // 2, width // 2)
        where = slice(start // 2, start // 2 + width // 2)
        for c in lgot[n]:
            c.wait_recv()
        rgot[n] = []
        for i, head in reversed(list(enumerate(HEADS))):
            spot = slice(16 * i, 16 * i + 16)
            value = kept[n][i] + leaf_in[0, spot, where].astype(F32) + leaf_in[1, spot, where].astype(F32)
            if head == 6:
                value = value + far_in[:, where].astype(F32)
            if head == 0:
                kept[n] = value
            else:
                relay_out[i - 1, :, where] = value.astype(BF)
                rgot[n].append(send(remote(
                    relay_out.at[i - 1, :, half], relay_in.at[i - 1, :, half],
                    rel_ss.at[4 * n + i - 1], rel_rs.at[4 * n + i - 1], xz(0, head),
                )))

    def finish(n):
        start, width = starts[n], 256 * len(CHUNKS[n])
        where = slice(start // 2, start // 2 + width // 2)
        for c in rgot[n]:
            c.wait_recv()
        value = kept[n]
        for i in range(4):
            value = value + relay_in[i, :, where].astype(F32)
        whole = jnp.concatenate([value[0:8], value[8:16]], axis=1)
        for m, distance in enumerate(CHUNKS[n]):
            column = pl.ds(pl.multiple_of(chip_of(distance) * 256, 256), 256)
            final[:, column] = (
                hid[:, column].astype(F32) + whole[:, 256 * m:256 * (m + 1)]
            ).astype(BF)

    for k in (0, 1):
        for way in (0, 1):
            gout.arrive(1, k, way)
    answer(0)
    for k in (0, 1):
        for way in (0, 1):
            gout.arrive(2, k, way)
    answer(1)
    spread(0)
    for k in (0, 1):
        for way in (0, 1):
            gout.arrive(3, k, way)
    relay(0)
    spread(1)
    gout.arrive(4, 0, 0)
    gout.arrive(4, 1, 1)
    answer(2)
    relay(1)
    spread(2)
    finish(0)
    finish(1)
    relay(2)
    finish(2)
    for c in sends:
        c.wait_send()


def per_device(learner_in, learner_out, placement, hidden, norm_gain, expert_ids, gate_weights):
    dma = pltpu.SemaphoreType.DMA
    vmem = pltpu.VMEM
    chunks = len(CHUNKS)
    rin, rout, final = pl.pallas_call(
        kernel,
        out_shape=(
            jax.ShapeDtypeStruct((2048, 1024), BF),
            jax.ShapeDtypeStruct((512, 2048), BF),
            jax.ShapeDtypeStruct((8, 2048), BF),
        ),
        in_specs=[pl.BlockSpec(memory_space=pl.ANY)] * 7,
        out_specs=[pl.BlockSpec(memory_space=pltpu.VMEM)] * 3,
        scratch_shapes=[
            vmem((128, 1024), BF), vmem((512, 128), BF), vmem((1, 64), jnp.int32), vmem((8, 2048), BF),
            vmem((1, 2048), F32), vmem((8, 10), jnp.int32), vmem((8, 10), F32),
            vmem((16, 16, 1152), BF), vmem((128, 2048), BF), vmem((128, 2048), BF),
            vmem((128, 1024), F32), vmem((256, 128), BF),
            vmem((128, 2048), BF), vmem((128, 2048), BF),
            vmem((2, 80, 1024), BF), vmem((2, 80, 1024), BF), vmem((16, 1024), BF), vmem((16, 1024), BF),
            vmem((4, 16, 1024), BF), vmem((4, 16, 1024), BF),
            dma((7,)),
            dma((14,)), dma((14,)), dma((14,)), dma((14,)),
            dma((16,)), dma((16,)), dma((16,)), dma((16,)),
            dma((16,)), dma((16,)), dma((4,)), dma((4,)),
            dma((3 * chunks,)), dma((3 * chunks,)), dma((2 * chunks,)), dma((2 * chunks,)),
            dma((chunks,)), dma((chunks,)), dma((4 * chunks,)), dma((4 * chunks,)),
        ],
        compiler_params=pltpu.CompilerParams(
            collective_id=0, has_side_effects=True, vmem_limit_bytes=40 * 2**20
        ),
    )(
        learner_in.reshape(128, 1024), learner_out.reshape(512, 128), placement.reshape(1, 64), hidden,
        norm_gain.reshape(1, 2048), expert_ids.reshape(8, 10), gate_weights.reshape(8, 10),
    )
    return rin[None], rout[None], final


def solution(mesh):
    in_specs = (
        P(("ep", "dp"), "fsdp", None),
        P(("ep", "dp"), None, "fsdp"),
        P(),
        P(("ep", "fsdp", "dp"), None),
        P(),
        P(None, ("ep", "fsdp", "dp"), None),
        P(None, ("ep", "fsdp", "dp"), None),
    )
    out_specs = (
        P(("ep", "dp"), None, None),
        P(("ep", "dp"), None, None),
        P(("ep", "fsdp", "dp"), None),
    )
    return jax.shard_map(
        per_device, mesh=mesh, in_specs=in_specs, out_specs=out_specs, check_vma=False
    )
```

time: 191 us -> 95.4 us (0.50)
  the two profiles are of different devices: /device:TPU:64 before, /device:TPU:16 now
where the time goes in v1:
time: 95.4 us; the launch traced here: 95 us
  Pallas kernels  85.1 us (89%)
  local copies, waits for them, and re-layouts  9.28 us (10%)
    pallas_call x1, Pallas kernels, per_device(): pl.pallas_call(kernel, out_shape=(jax.ShapeDtypeStruct((2048, 1024), BF),...  85.1 us
    unnamed x17, local copies, waits for them, and re-layouts  9.28 us

profile of v1, /device:TPU:16, one launch (start us, length us, event | category | flops | bytes accessed | tf_op | source)
XLA Modules:
  0.0 95.0 jit_solution(13047342943159898561)
XLA Ops:
  0.6 0.0 copy-start
  0.6 0.9 copy-done
  1.6 0.0 copy-start.1
  1.6 0.9 copy-done.1
  2.5 0.0 copy-start.2
  2.5 0.8 copy-done.2
  3.2 0.0 copy-start.3
  3.2 0.7 copy-done.3
  3.9 0.0 copy-start.4
  3.9 0.7 copy-done.4
  4.6 0.0 copy-start.5
  4.6 0.7 copy-done.5
  5.3 0.0 copy-start.6
  5.3 0.7 copy-done.6
  6.0 85.1 %shard_map.94 = (bf16[2048,1024]{1,0:T(8,128)(2,1)S(1)}, bf16[512,2048]{1,0:T(8,128)(2,1)S(1)}, bf16[8,2048]{1,0:T(8,128)(2,1)S(1)}) custom-call(bf16[128,1024]{1,0:T(8,128)(2,1)S(1)} %bitcast.10, bf16[512,128]{1,0:T(8,128)(2,1)S(1)} %bitcast.11, s32[1,64]{1,0:T(1,128)S(1)} %bitcast.15, bf16[8,2048]{1,0:T(8,128)(2,1)S(1)} %copy-done.2, ...), custom_call_target="tpu_custom_call" | custom-call | tf_op jit(solution)/shard_map/pallas_call | solution.py:419
  91.1 2.0 %copy.13 = bf16[1,2048,1024]{2,1,0:T(8,128)(2,1)} copy(bf16[1,2048,1024]{2,1,0:T(8,128)(2,1)S(1)} %bitcast.8) | data formatting | bytes 8388608
  93.1 1.3 %copy.14 = bf16[1,512,2048]{2,1,0:T(8,128)(2,1)} copy(bf16[1,512,2048]{2,1,0:T(8,128)(2,1)S(1)} %bitcast.9) | data formatting | bytes 4194304
  94.4 0.6 copy.15
Async XLA Ops:
  0.6 1.0 %copy-start = (bf16[1,128,1024]{2,1,0:T(8,128)(2,1)S(1)}, bf16[1,128,1024]{2,1,0:T(8,128)(2,1)}, u32[]{:S(2)}) copy-start(bf16[1,128,1024]{2,1,0:T(8,128)(2,1)} %param.7) | copy-start | bytes 786436
  1.6 0.9 copy-start.1
  2.5 0.8 copy-start.2
  3.2 0.7 copy-start.3
  3.9 0.7 copy-start.4
  4.6 0.7 copy-start.5
  5.3 0.7 copy-start.6

commit v2 on v1

--- a/solution.py
+++ b/solution.py
@@ -8,9 +8,10 @@
 MESH = pl.DeviceIdType.MESH
 BF, F32 = jnp.bfloat16, jnp.float32
 BLOCK = 128
-CHUNKS = ((0, 1, -1), (2, -2), (3, -3, 4))
-RELAYS = (3, -3, 6, -6)
+CHUNKS = ((0, 1, -1), (2, -2), (3, -3), (4,))
+STARTS = (0, 768, 1280, 1792)
 HEADS = (0, 3, -3, 6, -6)
+OFFSETS = (0, 1, -1, 2, -2, 3, -3, 4, -4, 5, -5, 6, -6, 7, -7, 8)
 
 
 def remote(src, dst, send_sem, recv_sem, device):
@@ -52,6 +53,10 @@
     return jnp.where(jnp.abs(block) >= scale * 2.0**-14, coarse, fine).astype(BF)
 
 
+def place_of(distance):
+    return OFFSETS.index((distance + 7) % 16 - 7)
+
+
 def fold(a):
     half = a.shape[1] // 2
     return jnp.concatenate([a[:, :half], a[:, half:]], axis=0)
@@ -62,10 +67,10 @@
     rin, rout, final,
     lin, lout, place, hid, gain, ids, gates,
     bundles, outgoing, arrived, acc, merge,
-    ans, back, leaf_out, leaf_in, far_out, far_in, relay_out, relay_in,
+    ans, back, leaf_out, leaf_in, far_out, far_in, relay_out, relay_in, last_out, last_in,
     load_sem,
     in_ss, in_rs, out_ss, out_rs, insib_ss, insib_rs, outsib_ss, outsib_rs,
-    z_ss, z_rs, x_ss, x_rs, bx_ss, bx_rs, leaf_ss, leaf_rs, far_ss, far_rs, rel_ss, rel_rs,
+    z_ss, z_rs, x_ss, x_rs, bx_ss, bx_rs, leaf_ss, leaf_rs, far_ss, far_rs, rel_ss, rel_rs, last_ss, last_rs,
 ):
     ep, dp, fs = lax.axis_index("ep"), lax.axis_index("dp"), lax.axis_index("fsdp")
     x, z = ep % 4, dp * 4 + ep // 4
@@ -89,7 +94,7 @@
 
     barrier = pltpu.get_barrier_semaphore()
     peers = [up, down, sibling] + [xz(d, 0) for d in (1, 2, 3)]
-    peers += [xz(0, d) for d in (1, -1, 2, -2, 3, -3, 6, -6)]
+    peers += [xz(0, d) for d in OFFSETS[1:]]
     for peer in peers:
         pl.semaphore_signal(barrier, inc=1, device_id=peer, device_id_type=MESH)
 
@@ -109,13 +114,14 @@
 
     def out_ref(distance, k, c):
         column = (chip_of(distance) * 2 + c) * 128
-        return rout.at[pl.ds(k * 256, 256), pl.ds(pl.multiple_of(column, 128), 128)]
+        return rout.at[pl.ds(k * 128, 128), pl.ds(pl.multiple_of(column, 128), 128)]
 
     ring = {}
 
     class Gather:
-        def __init__(self, ref, ss, rs, sib_ss, sib_rs):
-            self.ref, self.ss, self.rs, self.sib_ss, self.sib_rs = ref, ss, rs, sib_ss, sib_rs
+        def __init__(self, ref, pieces, ss, rs, sib_ss, sib_rs):
+            self.ref, self.pieces = ref, pieces
+            self.ss, self.rs, self.sib_ss, self.sib_rs = ss, rs, sib_ss, sib_rs
             self.got, self.sib = {}, {}
             self.n = 0
             self.m = 0
@@ -133,19 +139,30 @@
             self.m += 1
             self.sib[(distance, k)] = send(c)
 
-        def arrive(self, step, k, way):
-            self.got[(step, k, way)].wait_recv()
-            if step < 3 or (step == 3 and k == way):
-                self.push(step, k, way)
-            distance = -step if way == 0 else step
-            self.share(4 if step == 4 else distance, k)
+        def begin(self):
+            for k in range(self.pieces):
+                for way in (0, 1):
+                    self.push(0, k, way)
+
+        def begin_share(self):
+            for k in range(self.pieces):
+                self.share(0, k)
+
+        def arrive(self, step, k):
+            ways = (0, 1) if step < 4 else (int(k >= self.pieces // 2),)
+            for way in ways:
+                self.got[(step, k, way)].wait_recv()
+                if step < 3 or (step == 3 and way == int(k >= self.pieces // 2)):
+                    self.push(step, k, way)
+            for way in ways:
+                self.share(4 if step == 4 else (-step if way == 0 else step), k)
 
         def ready(self, distance):
-            for k in (0, 1):
+            for k in range(self.pieces):
                 self.sib[(distance, k)].wait_recv()
 
-    gin = Gather(in_ref, in_ss, in_rs, insib_ss, insib_rs)
-    gout = Gather(out_ref, out_ss, out_rs, outsib_ss, outsib_rs)
+    gin = Gather(in_ref, 2, in_ss, in_rs, insib_ss, insib_rs)
+    gout = Gather(out_ref, 4, out_ss, out_rs, outsib_ss, outsib_rs)
 
     loads[0].wait()
     peaks = []
@@ -161,11 +178,7 @@
                 block, scales[b:b + 1, :]
             )
     pl.semaphore_wait(barrier, len(peers))
-    for k in (0, 1):
-        for way in (0, 1):
-            gin.push(0, k, way)
-    for k in (0, 1):
-        gin.share(0, k)
+    gin.begin()
 
     for c in loads[1:6]:
         c.wait()
@@ -200,16 +213,15 @@
 
     zgot = {}
 
-    def zsend(held, hop, i):
-        there = (held - hop) % 16
+    def zsend(held, hop):
+        here, there = place_of(held), place_of(held - hop)
         zgot[there] = send(remote(
-            bundles.at[held % 16], bundles.at[there], z_ss.at[i], z_rs.at[i], xz(0, hop)
+            bundles.at[here], bundles.at[there], z_ss.at[there], z_rs.at[there], xz(0, hop)
         ))
 
-    for i, hop in enumerate((6, -6, 3, -3)):
-        zsend(0, hop, i)
-    zsend(0, 1, 4)
-    zsend(0, -1, 5)
+    for hop in (3, -3, 1, -1, 6, -6):
+        zsend(0, hop)
+    gin.begin_share()
 
     loads[6].wait()
     peaks = []
@@ -222,57 +234,62 @@
         for r in (0, 64):
             here = slice(b * BLOCK + r, b * BLOCK + r + 64)
             rout[here, own_column] = quantized(lout[here, :].astype(F32), scales[b:b + 1, :])
-    for k in (0, 1):
-        gout.share(0, k)
-
-    gin.arrive(1, 0, 0)
-    gin.arrive(1, 0, 1)
-    number = 6
-    for held in (3, -3, 6, -6):
-        zgot[held % 16].wait_recv()
+    gout.begin_share()
+
+    def relay_rows(held):
+        zgot[place_of(held)].wait_recv()
         for hop in (1, -1):
-            zsend(held, hop, number)
-            number += 1
+            zsend(held, hop)
         if held == 6:
-            zsend(held, -2, number)
-            number += 1
-    gin.arrive(1, 1, 0)
-    gin.arrive(1, 1, 1)
-    gin.arrive(2, 0, 0)
-    gin.arrive(2, 0, 1)
-
-    for offset in range(1, 16):
-        if offset not in (3, 13, 6, 10):
-            zgot[offset].wait_recv()
-    every = bundles[...].reshape(256, 1152)
-    table, held_rows = every[:, 1024:], every[:, :1024]
-    line, lane = iota((128, 128), 0), iota((128, 128), 1)
-    target = 4 * z + ((x + (line >> 5)) & 3)
+            zsend(held, -2)
+
+    xgot = []
+    line, lane = iota((64, 128), 0), iota((64, 128), 1)
+    target = 4 * z + ((x + (line >> 4)) & 3)
     pick = jnp.where(lane == target, 1.0, 0.0).astype(BF)
     pick_gate = jnp.where(lane == target + 64, 1.0, 0.0).astype(BF)
-    line, lane = iota((128, 256), 0), iota((128, 256), 1)
-    same = ((line >> 1) & 15) == (lane >> 4)
-    chosen = jnp.where(same, dot_t(pick, table), 0.0) == ((line & 1) + 1).astype(F32)
-    left = jnp.where(chosen, jnp.where((lane & 8) == 0, 1.0, 0.0), 0.0).astype(BF)
-    right = jnp.where(chosen, jnp.where((lane & 8) == 0, 0.0, 1.0), 0.0).astype(BF)
-    outgoing[:, 0:1024] = dot(left, held_rows).astype(BF)
-    outgoing[:, 1024:2048] = dot(right, held_rows).astype(BF)
-    xgot = []
-    for dx in (2, 1, 3):
-        block = pl.ds(dx * 32, 32)
-        xgot.append(send(remote(
-            outgoing.at[block, :], arrived.at[block, :], x_ss.at[dx], x_rs.at[dx], xz(dx, 0)
-        )))
-    arrived[0:32, :] = outgoing[0:32, :]
-    line, lane = iota((256, 128), 0), iota((256, 128), 1)
-    same = ((lane >> 1) & 15) == (line >> 4)
-    chosen = jnp.where(same, dot_t(table, pick), 0.0) == ((lane & 1) + 1).astype(F32)
-    merge[...] = jnp.where(chosen, dot_t(table, pick_gate), 0.0).astype(BF)
-
-    gin.arrive(2, 1, 0)
-    gin.arrive(2, 1, 1)
-    gin.arrive(3, 0, 0)
-    gin.arrive(3, 0, 1)
+
+    def select(half):
+        for distance in OFFSETS[8 * half:8 * half + 8]:
+            if distance not in HEADS:
+                zgot[place_of(distance)].wait_recv()
+        every = bundles[8 * half:8 * half + 8].reshape(128, 1152)
+        table, held_rows = every[:, 1024:], every[:, :1024]
+        line, lane = iota((64, 128), 0), iota((64, 128), 1)
+        same = ((line >> 1) & 7) == (lane >> 4)
+        chosen = jnp.where(same, dot_t(pick, table), 0.0) == ((line & 1) + 1).astype(F32)
+        left = jnp.where(chosen, jnp.where((lane & 8) == 0, 1.0, 0.0), 0.0).astype(BF)
+        right = jnp.where(chosen, jnp.where((lane & 8) == 0, 0.0, 1.0), 0.0).astype(BF)
+        rows_of = slice(64 * half, 64 * half + 64)
+        outgoing[rows_of, 0:1024] = dot(left, held_rows).astype(BF)
+        outgoing[rows_of, 1024:2048] = dot(right, held_rows).astype(BF)
+        for dx in (2, 1, 3):
+            block = pl.ds(64 * half + dx * 16, 16)
+            xgot.append(send(remote(
+                outgoing.at[block, :], arrived.at[block, :],
+                x_ss.at[4 * half + dx], x_rs.at[4 * half + dx], xz(dx, 0),
+            )))
+        arrived[64 * half:64 * half + 16, :] = outgoing[64 * half:64 * half + 16, :]
+        line, lane = iota((128, 64), 0), iota((128, 64), 1)
+        same = ((lane >> 1) & 7) == (line >> 4)
+        chosen = jnp.where(same, dot_t(table, pick), 0.0) == ((lane & 1) + 1).astype(F32)
+        merge[128 * half:128 * half + 128, :] = jnp.where(chosen, dot_t(table, pick_gate), 0.0).astype(BF)
+
+    gin.arrive(1, 0)
+    relay_rows(3)
+    relay_rows(-3)
+    gin.arrive(1, 1)
+    relay_rows(6)
+    relay_rows(-6)
+    gin.arrive(2, 0)
+    select(0)
+    gin.arrive(2, 1)
+    gin.arrive(3, 0)
+    select(1)
+    gin.arrive(3, 1)
+    gout.begin()
+    gin.arrive(4, 0)
+    gin.arrive(4, 1)
     for c in xgot:
         c.wait_recv()
 
@@ -286,52 +303,57 @@
             acc[...] += part
 
     project(0, True)
-    gin.arrive(3, 1, 0)
-    gin.arrive(3, 1, 1)
-    for k in (0, 1):
-        for way in (0, 1):
-            gout.push(0, k, way)
-    for distance in (1, -1, 2, -2, 3, -3):
+    for distance in (1, -1, 2, -2):
         project(distance)
-    gin.arrive(4, 0, 0)
-    gin.arrive(4, 1, 1)
+    gout.arrive(1, 0)
+    gout.arrive(1, 1)
+    for distance in (3, -3):
+        project(distance)
+    gout.arrive(1, 2)
+    gout.arrive(1, 3)
     project(4)
     gate, lift = acc[:, 0:512], acc[:, 512:1024]
     units = (gate / (1.0 + jnp.exp(-gate)) * lift).astype(BF)
 
-    starts, total = [], 0
-    for chunk in CHUNKS:
-        starts.append(total)
-        total += 256 * len(chunk)
     bgot, lgot, rgot, kept = {}, {}, {}, {}
 
     def answer(n):
-        chunk, start = CHUNKS[n], starts[n]
+        chunk, start = CHUNKS[n], STARTS[n]
         for m, distance in enumerate(chunk):
             gout.ready(distance)
             column = pl.multiple_of(chip_of(distance) * 256, 256)
-            ans[:, start + 256 * m:start + 256 * (m + 1)] = dot(
+            ans[:, :, start + 256 * m:start + 256 * (m + 1)] = dot(
                 units, rout[:, pl.ds(column, 256)]
-            ).astype(BF)
+            ).astype(BF).reshape(2, 64, 256)
         columns = pl.ds(start, 256 * len(chunk))
         bgot[n] = []
         for dx in (2, 1, 3):
-            block = pl.ds(dx * 32, 32)
+            block = pl.ds(dx * 16, 16)
             bgot[n].append(send(remote(
-                ans.at[block, columns], back.at[block, columns],
+                ans.at[:, block, columns], back.at[:, block, columns],
                 bx_ss.at[3 * n + dx - 1], bx_rs.at[3 * n + dx - 1], xz(-dx, 0),
             )))
-        back[0:32, start:start + 256 * len(chunk)] = ans[0:32, start:start + 256 * len(chunk)]
+        back[:, 0:16, start:start + 256 * len(chunk)] = ans[:, 0:16, start:start + 256 * len(chunk)]
 
     def spread(n):
-        start, width = starts[n], 256 * len(CHUNKS[n])
+        start, width = STARTS[n], 256 * len(CHUNKS[n])
         for c in bgot[n]:
             c.wait_recv()
-        sums = dot(merge[...], back[:, start:start + width])
-
-        def part(offset):
-            at = (offset % 16) * 16
-            return fold(sums[at:at + 8] + sums[at + 8:at + 16])
+        sums = [dot(merge[128 * b:128 * b + 128, :], back[b, :, start:start + width]) for b in (0, 1)]
+
+        def part(distance):
+            half, at = place_of(distance) // 8, place_of(distance) % 8 * 16
+            return fold(sums[half][at:at + 8] + sums[half][at + 8:at + 16])
+
+        if n == 3:
+            lgot[n] = []
+            for i in range(15, 0, -1):
+                last_out[i] = part(OFFSETS[i]).astype(BF)
+                lgot[n].append(send(remote(
+                    last_out.at[i], last_in.at[i], last_ss.at[i], last_rs.at[i], xz(0, OFFSETS[i])
+                )))
+            kept[n] = part(0)
+            return
 
         half = pl.ds(start // 2, width // 2)
         where = slice(start // 2, start // 2 + width // 2)
@@ -350,7 +372,7 @@
         kept[n] = [part(head) for head in HEADS]
 
     def relay(n):
-        start, width = starts[n], 256 * len(CHUNKS[n])
+        start, width = STARTS[n], 256 * len(CHUNKS[n])
         half = pl.ds(start // 2, width // 2)
         where = slice(start // 2, start // 2 + width // 2)
         for c in lgot[n]:
@@ -371,13 +393,13 @@
                 )))
 
     def finish(n):
-        start, width = starts[n], 256 * len(CHUNKS[n])
+        start, width = STARTS[n], 256 * len(CHUNKS[n])
         where = slice(start // 2, start // 2 + width // 2)
-        for c in rgot[n]:
+        for c in lgot[n] if n == 3 else rgot[n]:
             c.wait_recv()
         value = kept[n]
-        for i in range(4):
-            value = value + relay_in[i, :, where].astype(F32)
+        for got in [last_in[i] for i in range(1, 16)] if n == 3 else [relay_in[i, :, where] for i in range(4)]:
+            value = value + got.astype(F32)
         whole = jnp.concatenate([value[0:8], value[8:16]], axis=1)
         for m, distance in enumerate(CHUNKS[n]):
             column = pl.ds(pl.multiple_of(chip_of(distance) * 256, 256), 256)
@@ -385,29 +407,31 @@
                 hid[:, column].astype(F32) + whole[:, 256 * m:256 * (m + 1)]
             ).astype(BF)
 
-    for k in (0, 1):
-        for way in (0, 1):
-            gout.arrive(1, k, way)
+    gout.arrive(2, 0)
     answer(0)
-    for k in (0, 1):
-        for way in (0, 1):
-            gout.arrive(2, k, way)
+    gout.arrive(2, 1)
+    gout.arrive(2, 2)
+    gout.arrive(2, 3)
+    gout.arrive(3, 0)
     answer(1)
+    gout.arrive(3, 1)
     spread(0)
-    for k in (0, 1):
-        for way in (0, 1):
-            gout.arrive(3, k, way)
+    gout.arrive(3, 2)
+    gout.arrive(3, 3)
+    answer(2)
+    for k in range(4):
+        gout.arrive(4, k)
+    spread(1)
     relay(0)
-    spread(1)
-    gout.arrive(4, 0, 0)
-    gout.arrive(4, 1, 1)
-    answer(2)
+    answer(3)
+    spread(2)
+    spread(3)
     relay(1)
-    spread(2)
+    relay(2)
     finish(0)
     finish(1)
-    relay(2)
     finish(2)
+    finish(3)
     for c in sends:
         c.wait_send()
 
@@ -429,23 +453,24 @@
             vmem((128, 1024), BF), vmem((512, 128), BF), vmem((1, 64), jnp.int32), vmem((8, 2048), BF),
             vmem((1, 2048), F32), vmem((8, 10), jnp.int32), vmem((8, 10), F32),
             vmem((16, 16, 1152), BF), vmem((128, 2048), BF), vmem((128, 2048), BF),
-            vmem((128, 1024), F32), vmem((256, 128), BF),
-            vmem((128, 2048), BF), vmem((128, 2048), BF),
+            vmem((128, 1024), F32), vmem((256, 64), BF),
+            vmem((2, 64, 2048), BF), vmem((2, 64, 2048), BF),
             vmem((2, 80, 1024), BF), vmem((2, 80, 1024), BF), vmem((16, 1024), BF), vmem((16, 1024), BF),
             vmem((4, 16, 1024), BF), vmem((4, 16, 1024), BF),
+            vmem((16, 16, 128), BF), vmem((16, 16, 128), BF),
             dma((7,)),
-            dma((14,)), dma((14,)), dma((14,)), dma((14,)),
-            dma((16,)), dma((16,)), dma((16,)), dma((16,)),
-            dma((16,)), dma((16,)), dma((4,)), dma((4,)),
+            dma((14,)), dma((14,)), dma((28,)), dma((28,)),
+            dma((16,)), dma((16,)), dma((32,)), dma((32,)),
+            dma((16,)), dma((16,)), dma((8,)), dma((8,)),
             dma((3 * chunks,)), dma((3 * chunks,)), dma((2 * chunks,)), dma((2 * chunks,)),
-            dma((chunks,)), dma((chunks,)), dma((4 * chunks,)), dma((4 * chunks,)),
+            dma((chunks,)), dma((chunks,)), dma((4 * chunks,)), dma((4 * chunks,)), dma((16,)), dma((16,)),
         ],
         compiler_params=pltpu.CompilerParams(
             collective_id=0, has_side_effects=True, vmem_limit_bytes=40 * 2**20
         ),
     )(
-        learner_in.reshape(128, 1024), learner_out.reshape(512, 128), placement.reshape(1, 64), hidden,
-        norm_gain.reshape(1, 2048), expert_ids.reshape(8, 10), gate_weights.reshape(8, 10),
+        *[pltpu.with_memory_space_constraint(a, pltpu.HBM) for a in (learner_in.reshape(128, 1024), learner_out.reshape(512, 128), placement.reshape(1, 64), hidden,
+        norm_gain.reshape(1, 2048), expert_ids.reshape(8, 10), gate_weights.reshape(8, 10))]
     )
     return rin[None], rout[None], final
 

time: 95.4 us -> 86.3 us (0.905)
  the two profiles are of different devices: /device:TPU:16 before, /device:TPU:1 now
where the time goes in v2:
time: 86.3 us; the launch traced here: 86.1 us
  Pallas kernels  81.5 us (94%)
  local copies, waits for them, and re-layouts  3.95 us (5%)
    pallas_call x1, Pallas kernels, per_device(): pl.pallas_call(kernel, out_shape=(jax.ShapeDtypeStruct((2048, 1024), BF),...  81.5 us
    unnamed x3, local copies, waits for them, and re-layouts  3.95 us

profile of v2, /device:TPU:1, one launch (start us, length us, event | category | flops | bytes accessed | tf_op | source)
XLA Modules:
  0.0 86.1 jit_solution(16358218318896082205)
XLA Ops:
  0.6 81.5 %shard_map.94 = (bf16[2048,1024]{1,0:T(8,128)(2,1)S(1)}, bf16[512,2048]{1,0:T(8,128)(2,1)S(1)}, bf16[8,2048]{1,0:T(8,128)(2,1)S(1)}) custom-call(bf16[128,1024]{1,0:T(8,128)(2,1)} %bitcast.10, bf16[512,128]{1,0:T(8,128)(2,1)} %bitcast.11, s32[1,64]{1,0:T(1,128)} %bitcast.15, bf16[8,2048]{1,0:T(8,128)(2,1)} %hid_hbm.1, f32[1,2048]{1,0:T(1,128)} %bitcast.12, ...), custom_call_target="tpu_custom_call" | custom-call | tf_op jit(solution)/shard_map/pallas_call | solution.py:443
  82.2 2.0 %copy.13 = bf16[1,2048,1024]{2,1,0:T(8,128)(2,1)} copy(bf16[1,2048,1024]{2,1,0:T(8,128)(2,1)S(1)} %bitcast.8) | data formatting | bytes 8388608
  84.2 1.3 %copy.14 = bf16[1,512,2048]{2,1,0:T(8,128)(2,1)} copy(bf16[1,512,2048]{2,1,0:T(8,128)(2,1)S(1)} %bitcast.9) | data formatting | bytes 4194304
  85.5 0.6 copy.15
